TPU v7x, 256 devices: a whole 4x4x8 slice. The times are simulated.
256 devices in a mesh: blk: 32 (over y_hi, z, core), lag: 8 (over y_lo, x).
Axes of the slice: x: 4, y: 4 (y_hi: 2, y_lo: 2; y = y_hi * 2 + y_lo), z: 8, core: 2. Of those that a mesh axis runs over, the one named last changes fastest.
Arguments:
- waves: bfloat16 [1024, 4096], P('blk', 'lag'), may hold values from -6 to 6
- dest_of: int32 [1024], P('blk'), may hold values from 0 to 1023, as said below
- pair_mask: int32 [1024, 1024], P('blk'), may hold values from 0 to 1, as said below
Outputs:
- xcorr: float32 [1024, 512, 1024], P('blk', 'lag')
Inputs may be any that keep to these rules, and one draw needn't show every extreme that they name: dest_of is a permutation; position p belongs to owner p // 32; each owner receives exactly 1 stations from each source block of 32 stations, and those from source block s take positions s * 1 to s + 1 - 1 of the owner's tile. `pair_mask`: whole blocks of 32 x 32 aligned positions may be zero.
All inputs are finite; a program needn't handle non-finite values.
Results may differ from a plain program's by a relative error of at most 0.0041.
Values may be sent and summed in bfloat16 or wider, within the bound.
A program may use at most 192 MiB of HBM per device.

v0:
```python
import functools

import jax
import jax.numpy as jnp
from jax import lax
from jax.sharding import PartitionSpec as P
import jax.experimental.pallas as pl
import jax.experimental.pallas.tpu as pltpu

EPS = 1e-06
LAGS = 512
MESH = pl.DeviceIdType.MESH
SIZES = {"x": 4, "y": 4, "z": 8}


def gather_kernel(w_ref, d_ref, held, send, land, a_send, a_recv, s_sem, r_sem):
    b, g = lax.axis_index("blk"), lax.axis_index("lag")
    core, cz, yh = b % 2, (b // 2) % 8, b // 16
    yl, cx = g // 4, g % 4
    here = {"x": cx, "y": yh * 2 + yl, "z": cz}
    everywhere, upper, lower = pl.ds(0, 32), pl.ds(0, 16), pl.ds(16, 16)

    def device(pos, c):
        return ((pos["y"] // 2 * 8 + pos["z"]) * 2 + c, pos["y"] % 2 * 4 + pos["x"])

    def shifted(axis, by):
        n = SIZES[axis]
        return lax.rem(here[axis] + (by + n), n)

    def neighbour(axis, by):
        return device({**here, axis: shifted(axis, by)}, core)

    sibling = device(here, 1 - core)

    def slot(c, tiles, rows, x=None, y=None, z=None, y_low=None):
        low = slice(None) if y is None else y % 2
        return held.at[
            low if y_low is None else y_low,
            slice(None) if x is None else x,
            tiles,
            slice(None) if y is None else y // 2,
            slice(None) if z is None else z,
            c,
            rows,
        ]

    barrier = pltpu.get_barrier_semaphore()

    def greet_blk(i, _):
        pl.semaphore_signal(barrier, inc=1, device_id=(lax.rem(b + i, 32), g), device_id_type=MESH)
        return 0

    lax.fori_loop(1, 32, greet_blk, 0)
    for axis in "xy":
        for by in (1, 2, 3):
            if axis == "y" and by == 2:
                continue
            pl.semaphore_signal(barrier, inc=1, device_id=neighbour(axis, by), device_id_type=MESH)

    owner = d_ref[...] // 32
    pick = (lax.broadcasted_iota(jnp.int32, (32, 32), 0) == owner).astype(jnp.bfloat16)
    ordered = jnp.dot(pick, w_ref[...], preferred_element_type=jnp.float32).astype(jnp.bfloat16)
    source = lax.broadcasted_iota(jnp.int32, (512, 512), 0)
    target = lax.broadcasted_iota(jnp.int32, (512, 512), 1)
    apart = (source == target % 256 * 2 + target // 256).astype(jnp.bfloat16)
    ordered = jnp.dot(ordered, apart, preferred_element_type=jnp.float32)
    for k in range(4):
        send[:, k, :] = ordered[:, 128 * k : 128 * k + 128]
    pl.semaphore_wait(barrier, 36)

    def put(i, _):
        to = lax.rem(b + i, 32)
        pltpu.make_async_remote_copy(
            src_ref=send.at[to], dst_ref=land.at[b], send_sem=a_send, recv_sem=a_recv,
            device_id=(to, g), device_id_type=MESH,
        ).start()
        return 0

    lax.fori_loop(1, 32, put, 0)
    land[b] = send[b]
    every = pltpu.make_async_remote_copy(
        src_ref=send.at[pl.ds(0, 31)], dst_ref=land.at[pl.ds(0, 31)], send_sem=a_send, recv_sem=a_recv,
        device_id=sibling, device_id_type=MESH,
    )
    every.wait_recv()
    for k in range(4):
        held[yl, cx, k, yh, cz, core] = land[:, k, :].astype(jnp.bfloat16)

    pending, crossing, used = [], [], []

    def start(ref, to):
        index = len(used)
        used.append(index)
        copy = pltpu.make_async_remote_copy(
            src_ref=ref, dst_ref=ref, send_sem=s_sem.at[index], recv_sem=r_sem.at[index],
            device_id=to, device_id_type=MESH,
        )
        copy.start()
        pending.append(copy)
        return index

    def arrive(ref, index):
        pltpu.make_async_remote_copy(
            src_ref=ref, dst_ref=ref, send_sem=s_sem.at[index], recv_sem=r_sem.at[index],
            device_id=sibling, device_id_type=MESH,
        ).wait_recv()

    def across(**where):
        index = start(slot(core, **where), sibling)
        crossing.append((slot(1 - core, **where), index))

    def straight(axis, tiles, rows, **where):
        waits = []
        for by in (2, 1, 3) if axis != "z" else (4, 3, 5, 2, 6, 1, 7):
            index = start(slot(core, tiles, rows, **{**where, axis: here[axis]}), neighbour(axis, by))
            waits.append((slot(core, tiles, rows, **{**where, axis: shifted(axis, -by)}), index))
        return waits

    def settle(waits):
        for ref, index in waits:
            arrive(ref, index)

    first = pl.ds(0, 3)
    along_x = straight("x", 3, everywhere, y=here["y"], z=cz)
    along_z = straight("z", first, everywhere, x=cx, y=here["y"])
    settle(along_x)
    z_waits = straight("y", 3, everywhere, z=cz)
    settle(along_z)
    x_waits = straight("y", 0, everywhere, x=cx) + straight("y", 1, upper, x=cx)
    y_waits = straight("x", 2, everywhere, y=here["y"]) + straight("x", 1, lower, y=here["y"])

    own = {"x": [(0, upper), (0, lower), (1, upper)], "y": [(2, upper), (2, lower), (1, lower)], "z": [(3, upper), (3, lower)]}
    whole = {"x": [(0, everywhere), (1, upper)], "y": [(2, everywhere), (1, lower)], "z": [(3, everywhere)]}
    tickets = {}

    def launch(axis, piece, way, step, **part):
        tiles, rows = own[axis][piece]
        at = shifted(axis, -way * (step - 1))
        tickets[axis, piece, way, step] = start(slot(core, tiles, rows, **{axis: at}, **part), neighbour(axis, way))

    def landed(axis, piece, way, step, **part):
        tiles, rows = own[axis][piece]
        at = shifted(axis, -way * step)
        arrive(slot(core, tiles, rows, **{axis: at}, **part), tickets[axis, piece, way, step])

    def cross(axis, which, by):
        tiles, rows = whole[axis][which]
        across(tiles=tiles, rows=rows, **{axis: shifted(axis, by)})

    def begin(axis, waits):
        settle(waits)
        for piece in range(len(own[axis])):
            for way in (1, -1):
                launch(axis, piece, way, 1)
        for which in range(len(whole[axis])):
            cross(axis, which, 0)

    def z_round(piece, step):
        for way in (1, -1):
            landed("z", piece, way, step)
            if step < 3 or (way > 0) == (piece == 0):
                launch("z", piece, way, step + 1)

    def split(axis, way):
        if axis == "x":
            return {"y_low": 0 if way > 0 else 1}
        return {"x": pl.ds(0, 2) if way > 0 else pl.ds(2, 2)}

    def xy_round(axis, piece):
        for way in (1, -1):
            landed(axis, piece, way, 1)
            if piece == 2:
                launch(axis, piece, way, 2, **split(axis, way))
            elif (way > 0) == (piece == 0):
                launch(axis, piece, way, 2)

    begin("z", z_waits)
    begin("x", x_waits)
    begin("y", y_waits)
    z_round(0, 1)
    xy_round("x", 0)
    xy_round("y", 0)
    z_round(1, 1)
    cross("z", 0, 1)
    cross("z", 0, -1)
    z_round(0, 2)
    xy_round("x", 1)
    xy_round("y", 1)
    for axis in "xy":
        cross(axis, 0, 1)
        cross(axis, 0, -1)
    z_round(1, 2)
    cross("z", 0, 2)
    cross("z", 0, -2)
    z_round(0, 3)
    xy_round("x", 2)
    xy_round("y", 2)
    for axis in "xy":
        cross(axis, 1, 1)
        cross(axis, 1, -1)
    z_round(1, 3)
    cross("z", 0, 3)
    cross("z", 0, -3)
    for axis in "xy":
        landed(axis, 0, 1, 2)
        landed(axis, 1, -1, 2)
        cross(axis, 0, 2)
    landed("z", 0, 1, 4)
    landed("z", 1, -1, 4)
    cross("z", 0, 4)
    for axis in "xy":
        for way in (1, -1):
            landed(axis, 2, way, 2, **split(axis, way))
        cross(axis, 1, 2)
    for ref, index in crossing:
        arrive(ref, index)
    every.wait_send()
    for copy in pending:
        copy.wait_send()


def gather(waves, dest_of):
    count = 96
    return pl.pallas_call(
        gather_kernel,
        out_shape=pltpu.VMEM((2, 4, 4, 2, 8, 2, 32, 128), jnp.bfloat16),
        in_specs=[pl.BlockSpec(memory_space=pltpu.VMEM)] * 2,
        out_specs=pl.BlockSpec(memory_space=pltpu.VMEM),
        scratch_shapes=[
            pltpu.VMEM((32, 4, 128), jnp.float32),
            pltpu.VMEM((32, 4, 128), jnp.float32),
            pltpu.SemaphoreType.DMA,
            pltpu.SemaphoreType.DMA,
            pltpu.SemaphoreType.DMA((count,)),
            pltpu.SemaphoreType.DMA((count,)),
        ],
        compiler_params=pltpu.CompilerParams(
            collective_id=0, has_side_effects=True, vmem_limit_bytes=32 * 2**20
        ),
    )(waves, dest_of)


CONTRACT = (((1,), (1,)), ((), ()))


def correlate_kernel(g_ref, m_ref, o_ref, even_rows, odd_rows, sums, scale_ref, e_ref, stage, sem):
    blk, lag = lax.axis_index("blk"), lax.axis_index("lag")

    def shift():
        tile = pl.ds(pl.multiple_of(32 * blk, 32), 32)
        pick = lambda first: jnp.concatenate(
            [g_ref[4 * g + first + k, tile, :].astype(jnp.float32) for g in range(8) for k in (0, 1)], axis=1
        )
        even, odd = pick(0), pick(2)
        mean_square = jnp.sum(even * even + odd * odd, axis=1, keepdims=True) * (1.0 / 4096)
        factor = lax.rsqrt(mean_square + EPS)
        edge = jnp.zeros((32, 256), jnp.float32)
        extend = lambda x: jnp.concatenate(
            [edge, (x * factor).astype(jnp.bfloat16).astype(jnp.float32), edge], axis=1
        )
        even, odd = extend(even), extend(odd)
        by = 2304 + 32 * lag
        before = pltpu.roll(odd, by + 1, 1)[:, :2176]
        even, odd = pltpu.roll(even, by, 1)[:, :2176], pltpu.roll(odd, by, 1)[:, :2176]
        e_ref[0] = even
        e_ref[1] = odd - even
        e_ref[2] = before - even

    def build(chunk, rows_ref):
        for q in range(8):
            for kind in (1, 2, 0):
                x = jnp.broadcast_to(e_ref[kind, 8 * chunk + q : 8 * chunk + q + 1, :], (8, 2176))
                for half in range(2):
                    y = [pltpu.roll(x, 16 * half + 8 * e, 1, stride=1, stride_axis=0)[:, 128:] for e in (0, 1)]
                    at = 32 * q + 16 * half
                    rows_ref[kind, at : at + 16, :] = jnp.concatenate(y, 0).astype(jnp.bfloat16)

    def prepare(n):
        totals = []
        for r in range(4):
            rows = slice(256 * n + 64 * r, 256 * n + 64 * r + 64)
            total = jnp.zeros((64, 128), jnp.float32)
            for g in range(8):
                for lane in range(2):
                    v0 = g_ref[4 * g + lane, rows, :].astype(jnp.float32)
                    v1 = g_ref[4 * g + 2 + lane, rows, :].astype(jnp.float32)
                    sums[g, rows, 128 * lane : 128 * lane + 128] = (v0 + v1).astype(jnp.bfloat16)
                    total += v0 * v0 + v1 * v1
            totals.append(total)
        square = lax.dot_general(
            jnp.ones((8, 128), jnp.float32), jnp.concatenate(totals, 0), CONTRACT,
            precision=lax.Precision.HIGHEST, preferred_element_type=jnp.float32,
        )
        scale_ref[:, 256 * n : 256 * n + 256] = lax.rsqrt(square * (1.0 / 4096) + EPS) * (1.0 / 64)

    def columns(n, kind, g):
        rows = slice(256 * n, 256 * n + 256)
        if kind == 0:
            return sums[g, rows, :]
        first = 4 * g + (2 if kind == 1 else 0)
        return jnp.concatenate([g_ref[first, rows, :], g_ref[first + 1, rows, :]], axis=1)

    def away(chunk, tile):
        return pltpu.make_async_copy(
            stage.at[chunk % 2, tile],
            o_ref.at[pl.ds(8 * chunk, 8), :, pl.ds(128 * tile, 128)],
            sem.at[chunk % 2, tile],
        )

    def multiply(chunk, rows_ref):
        if chunk >= 2:
            for tile in range(8):
                away(chunk - 2, tile).wait()
        for n in range(4):
            if chunk == 0:
                prepare(n)
            products = {}
            for kind in (1, 2, 0):
                right = jnp.concatenate([columns(n, kind, g) for g in range(8)], axis=1)
                products[kind] = lax.dot_general(
                    rows_ref[kind], right, CONTRACT, preferred_element_type=jnp.float32
                )
            for c in range(2):
                cols = slice(256 * n + 128 * c, 256 * n + 128 * c + 128)
                lanes = slice(128 * c, 128 * c + 128)
                for q in range(8):
                    part = slice(32 * q, 32 * q + 32)
                    a = 8 * chunk + q
                    factor = m_ref[a : a + 1, cols].astype(jnp.float32) * scale_ref[0:1, cols]
                    for p in range(2):
                        value = (products[0][part, lanes] + products[1 + p][part, lanes]) * factor
                        stage[chunk % 2, 2 * n + c, q, pl.ds(p, 32, stride=2), :] = value
                away(chunk, 2 * n + c).start()

    shift()
    build(0, even_rows)
    for chunk in range(4):
        now, later = (even_rows, odd_rows) if chunk % 2 == 0 else (odd_rows, even_rows)
        if chunk < 3:
            build(chunk + 1, later)
        multiply(chunk, now)
    for chunk in (2, 3):
        for tile in range(8):
            away(chunk, tile).wait()


def correlate(everyone, pair_mask):
    return pl.pallas_call(
        correlate_kernel,
        out_shape=jax.ShapeDtypeStruct((32, 64, 1024), jnp.float32),
        in_specs=[pl.BlockSpec(memory_space=pltpu.VMEM)] * 2,
        out_specs=pl.BlockSpec(memory_space=pl.ANY),
        scratch_shapes=[
            pltpu.VMEM((3, 256, 2048), jnp.bfloat16),
            pltpu.VMEM((3, 256, 2048), jnp.bfloat16),
            pltpu.VMEM((8, 1024, 256), jnp.bfloat16),
            pltpu.VMEM((8, 1024), jnp.float32),
            pltpu.VMEM((3, 32, 2176), jnp.float32),
            pltpu.VMEM((2, 8, 8, 64, 128), jnp.float32),
            pltpu.SemaphoreType.DMA((2, 8)),
        ],
        compiler_params=pltpu.CompilerParams(vmem_limit_bytes=40 * 2**20),
    )(everyone, pair_mask)


def body(waves, dest_of, pair_mask):
    everyone = gather(waves, dest_of[None, :]).reshape(32, 1024, 128)
    return correlate(everyone, pair_mask)


def solution(mesh):
    in_specs = (P("blk", "lag"), P("blk"), P("blk", None))
    out_specs = P("blk", "lag", None)
    return jax.shard_map(body, mesh=mesh, in_specs=in_specs, out_specs=out_specs, check_vma=False)
```

profile of v0, /device:TPU:1, one launch (start us, length us, event | category | flops | bytes accessed | tf_op | source)
XLA Modules:
  0.0 71.6 jit_solution(1518342189888805078)
XLA Ops:
  0.0 0.0 copy-start
  0.0 0.0 copy-start.1
  0.0 0.8 %copy-done.1 = bf16[32,512]{1,0:T(8,128)(2,1)S(1)} copy-done((bf16[32,512]{1,0:T(8,128)(2,1)S(1)}, bf16[32,512]{1,0:T(8,128)(2,1)}, u32[]{:S(2)}) %copy-start.1) | copy-done | bytes 32792
  0.8 0.0 copy-start.2
  0.8 0.7 copy-done.2
  1.5 51.9 %shard_map.37 = bf16[2,4,4,2,8,2,32,128]{7,6,5,4,3,2,1,0:T(8,128)(2,1)S(1)} custom-call(bf16[32,512]{1,0:T(8,128)(2,1)S(1)} %copy-done.1, s32[1,32]{1,0:T(1,128)S(1)} %bitcast.3), custom_call_target="tpu_custom_call" | custom-call | tf_op jit(solution)/shard_map/pallas_call | solution.py:224
  53.3 0.0 copy-done
  53.3 18.1 %shard_map.38 = f32[32,64,1024]{2,1,0:T(8,128)} custom-call(bf16[32,1024,128]{2,1,0:T(8,128)(2,1)S(1)} %bitcast.2, s32[32,1024]{1,0:T(8,128)S(1)} %copy-done), custom_call_target="tpu_custom_call" | custom-call | tf_op jit(solution)/shard_map/pallas_call | solution.py:348
Async XLA Ops:
  0.0 53.3 %copy-start = (s32[32,1024]{1,0:T(8,128)S(1)}, s32[32,1024]{1,0:T(8,128)}, u32[]{:S(2)}) copy-start(s32[32,1024]{1,0:T(8,128)} %m_ref.1) | copy-start | bytes 393220
  0.0 0.8 %copy-start.1 = (bf16[32,512]{1,0:T(8,128)(2,1)S(1)}, bf16[32,512]{1,0:T(8,128)(2,1)}, u32[]{:S(2)}) copy-start(bf16[32,512]{1,0:T(8,128)(2,1)} %w_ref.1) | copy-start | bytes 98308
  0.8 0.7 copy-start.2
where the time goes:
time: 71.7 us; the launch traced here: 71.6 us
  Pallas kernels  70 us (98%)
  local copies, waits for them, and re-layouts  1.45 us (2%)
    pallas_call x1, Pallas kernels, gather(): pl.pallas_call(gather_kernel, out_shape=pltpu.VMEM((2, 4, 4, 2, 8, 2, 32,...  51.9 us
    pallas_call x1, Pallas kernels, correlate(): pl.pallas_call(correlate_kernel, out_shape=jax.ShapeDtypeStruct((32, 64,...  18.1 us
    unnamed x6, local copies, waits for them, and re-layouts  1.45 us

commit v1 on v0

v1 whole, which is shorter than its diff:
```python
import functools

import jax
import jax.numpy as jnp
from jax import lax
from jax.sharding import PartitionSpec as P
import jax.experimental.pallas as pl
import jax.experimental.pallas.tpu as pltpu

EPS = 1e-06
LAGS = 512
MESH = pl.DeviceIdType.MESH
SIZES = {"x": 4, "y": 4, "z": 8}


def gather_kernel(w_hbm, d_hbm, held_x, held_y, held_z, w_ref, d_ref, in_sem, s_sem, r_sem):
    b, g = lax.axis_index("blk"), lax.axis_index("lag")
    core, cz, yh = b % 2, (b // 2) % 8, b // 16
    yl, cx = g // 4, g % 4
    cy = yh * 2 + yl
    here = {"x": cx, "y": cy, "z": cz}

    def device(pos, c):
        return ((pos["y"] // 2 * 8 + pos["z"]) * 2 + c, pos["y"] % 2 * 4 + pos["x"])

    def shifted(axis, by):
        n = SIZES[axis]
        return lax.rem(here[axis] + (by + n), n)

    def neighbour(axis, by):
        return device({**here, axis: shifted(axis, by)}, core)

    sibling = device(here, 1 - core)

    barrier = pltpu.get_barrier_semaphore()
    for axis in "xyz":
        for by in range(1, SIZES[axis]):
            pl.semaphore_signal(barrier, inc=1, device_id=neighbour(axis, by), device_id_type=MESH)
    pl.semaphore_signal(barrier, inc=1, device_id=sibling, device_id_type=MESH)

    fetch = [
        pltpu.make_async_copy(w_hbm, w_ref, in_sem.at[0]),
        pltpu.make_async_copy(d_hbm, d_ref, in_sem.at[1]),
    ]
    for copy in fetch:
        copy.start()
    source = lax.broadcasted_iota(jnp.int32, (512, 512), 0)
    target = lax.broadcasted_iota(jnp.int32, (1, 512), 1)
    apart = (source == target % 256 * 2 + target // 256).astype(jnp.bfloat16)
    to = lax.broadcasted_iota(jnp.int32, (256, 1), 0)
    of = lax.broadcasted_iota(jnp.int32, (1, 256), 1)
    place = lambda r: r // 16 % 8 * 2 + r // 128
    swap = ((place(to) == of % 16) & (to % 16 == place(of))).astype(jnp.bfloat16)
    for copy in fetch:
        copy.wait()
    owner = d_ref[...] // 32
    pick = (lax.broadcasted_iota(jnp.int32, (32, 32), 0) == owner).astype(jnp.bfloat16)
    ordered = jnp.dot(pick, w_ref[...], preferred_element_type=jnp.float32).astype(jnp.bfloat16)
    ordered = jnp.dot(ordered, apart, preferred_element_type=jnp.float32).astype(jnp.bfloat16)
    for k in range(3):
        held_x[core, cx, cy, cz, k] = ordered[:16, 128 * k : 128 * k + 128]
        held_y[core, cy, cx, cz, k] = ordered[16:, 128 * k : 128 * k + 128]
    for e in range(2):
        held_z[core, cz, cy, cx, e] = ordered[16 * e : 16 * e + 16, 384:]
    pl.semaphore_wait(barrier, 14)

    pending, used = {}, []

    def start(ref, to, unit):
        index = len(used)
        used.append(index)
        copy = pltpu.make_async_remote_copy(
            src_ref=ref, dst_ref=ref, send_sem=s_sem.at[index], recv_sem=r_sem.at[index],
            device_id=to, device_id_type=MESH,
        )
        copy.start()
        pending.setdefault(unit, []).append(copy)
        return index

    def arrive(ref, index):
        pltpu.make_async_remote_copy(
            src_ref=ref, dst_ref=ref, send_sem=s_sem.at[index], recv_sem=r_sem.at[index],
            device_id=sibling, device_id_type=MESH,
        ).wait_recv()

    def straight(unit, axis, ref_at):
        waits = {}
        for by in (2, 1, 3) if axis != "z" else (4, 3, 5, 2, 6, 1, 7):
            index = start(ref_at(here[axis]), neighbour(axis, by), (unit, 0))
            waits[by] = (ref_at(shifted(axis, -by)), index)
        return waits

    def settle(waits):
        for ref, index in waits.values():
            arrive(ref, index)

    crossing, tickets = {}, {}

    def piece_of(axis, at, piece):
        if axis == "x":
            return held_x.at[core, at, shifted("y", -piece)]
        if axis == "y":
            return held_y.at[core, at, shifted("x", -piece)]
        return held_z.at[core, at, pl.ds(2 * piece, 2)]

    def launch(axis, piece, way, step):
        at = shifted(axis, -way * (step - 1))
        unit = (axis, 0 if axis == "z" else -way * (step - 1))
        tickets[axis, piece, way, step] = start(piece_of(axis, at, piece), neighbour(axis, way), unit)

    def landed(axis, piece, way, step):
        arrive(piece_of(axis, shifted(axis, -way * step), piece), tickets[axis, piece, way, step])

    def begin(axis, piece):
        for way in (1, -1):
            launch(axis, piece, way, 1)

    def cross(axis, by):
        held = {"x": held_x, "y": held_y, "z": held_z}[axis]
        at = shifted(axis, by)
        index = start(held.at[core, at], sibling, (axis, 0 if axis == "z" else by))
        crossing[axis, by] = (held.at[1 - core, at], index)

    def z_round(piece, step):
        for way in (1, -1):
            landed("z", piece, way, step)
            if step < 3 or (way > 0) == (piece == 0):
                launch("z", piece, way, step + 1)

    forward = {0: 1, 1: -1, 2: 1, 3: -1}

    def xy_round(axis, piece):
        for way in (1, -1):
            landed(axis, piece, way, 1)
            if way == forward[piece]:
                launch(axis, piece, way, 2)

    def turn(views):
        joined = jnp.concatenate([ref[index].reshape(256, 128) for ref, index in views], axis=1)
        turned = jnp.dot(swap, joined, preferred_element_type=jnp.float32).astype(jnp.bfloat16)
        for k, (ref, index) in enumerate(views):
            ref[index] = turned[:, 128 * k : 128 * k + 128].reshape(2, 8, 16, 128)

    def ready(axis, bys):
        for by in bys:
            arrive(*crossing[axis, by])
        for by in bys if axis != "z" else (0,):
            for copy in pending.pop((axis, by)):
                copy.wait_send()

    def arrange(axis, by):
        ready(axis, (by,))
        held = held_x if axis == "x" else held_y
        at = shifted(axis, by)
        for part in range(2):
            turn([(held, (slice(None), at, 2 * part + near, slice(None), k)) for near in range(2) for k in range(3)])

    def arrange_z():
        ready("z", (0, 1, -1, 2, -2, 3, -3, 4))
        for y in range(4):
            turn([(held_z, (slice(None), slice(None), y, x, e)) for x in range(4) for e in range(2)])

    z_first = straight("z", "x", lambda at: held_z.at[core, cz, cy, at])
    x_first = straight("x", "z", lambda at: held_x.at[core, cx, cy, at])
    y_first = straight("y", "z", lambda at: held_y.at[core, cy, cx, at])
    settle(z_first)
    z_mid = straight("z", "y", lambda at: held_z.at[core, cz, at])
    settle(x_first)
    x_mid = straight("x", "y", lambda at: held_x.at[core, cx, at])
    begin("x", 0)
    settle(y_first)
    y_mid = straight("y", "x", lambda at: held_y.at[core, cy, at])
    begin("y", 0)
    settle(z_mid)
    begin("z", 0)
    begin("z", 1)
    cross("z", 0)
    for by in (1, 3, 2):
        arrive(*x_mid[by])
        begin("x", by)
    cross("x", 0)
    for by in (1, 3, 2):
        arrive(*y_mid[by])
        begin("y", by)
    cross("y", 0)
    z_round(0, 1)
    z_round(1, 1)
    cross("z", 1)
    cross("z", -1)
    xy_round("x", 0)
    xy_round("y", 0)
    z_round(0, 2)
    z_round(1, 2)
    cross("z", 2)
    cross("z", -2)
    xy_round("x", 1)
    xy_round("y", 1)
    z_round(0, 3)
    z_round(1, 3)
    cross("z", 3)
    cross("z", -3)
    xy_round("x", 3)
    xy_round("y", 3)
    xy_round("x", 2)
    cross("x", 1)
    cross("x", -1)
    xy_round("y", 2)
    cross("y", 1)
    cross("y", -1)
    arrange("x", 0)
    arrange("y", 0)
    landed("z", 0, 1, 4)
    landed("z", 1, -1, 4)
    cross("z", 4)
    for axis in "xy":
        arrange(axis, 1)
        arrange(axis, -1)
    for axis in "xy":
        for piece in (0, 1, 3, 2):
            landed(axis, piece, forward[piece], 2)
        cross(axis, 2)
    arrange_z()
    for axis in "xy":
        arrange(axis, 2)


def gather(waves, dest_of):
    count = 96
    return pl.pallas_call(
        gather_kernel,
        out_shape=[
            pltpu.VMEM((2, 4, 4, 8, 3, 16, 128), jnp.bfloat16),
            pltpu.VMEM((2, 4, 4, 8, 3, 16, 128), jnp.bfloat16),
            pltpu.VMEM((2, 8, 4, 4, 2, 16, 128), jnp.bfloat16),
        ],
        in_specs=[pl.BlockSpec(memory_space=pltpu.HBM)] * 2,
        out_specs=[pl.BlockSpec(memory_space=pltpu.VMEM)] * 3,
        scratch_shapes=[
            pltpu.VMEM((32, 512), jnp.bfloat16),
            pltpu.VMEM((1, 32), jnp.int32),
            pltpu.SemaphoreType.DMA((2,)),
            pltpu.SemaphoreType.DMA((count,)),
            pltpu.SemaphoreType.DMA((count,)),
        ],
        compiler_params=pltpu.CompilerParams(
            collective_id=0, has_side_effects=True, vmem_limit_bytes=16 * 2**20
        ),
    )(pltpu.with_memory_space_constraint(waves, pltpu.HBM), pltpu.with_memory_space_constraint(dest_of, pltpu.HBM))


CONTRACT = (((1,), (1,)), ((), ()))


def correlate_kernel(x_ref, y_ref, z_ref, m_hbm, o_ref, m_ref, m_sem, even_rows, odd_rows, sums, scale_ref, e_ref, stage, sem):
    blk, lag = lax.axis_index("blk"), lax.axis_index("lag")

    def shift():
        near, z, high = blk % 2, blk // 2 % 8, blk // 16

        def pick(first):
            lanes = []
            for g in range(8):
                for k in (first, first + 1):
                    x, rows = g % 4, []
                    for y in (g // 4, 2 + g // 4):
                        if k == 3:
                            rows.append(z_ref[near, z, y, x, high].astype(jnp.float32))
                        else:
                            a = x_ref[near, x, y, z, k].astype(jnp.float32)
                            b = y_ref[near, y, x, z, k].astype(jnp.float32)
                            rows.append(jnp.where(high == 0, a, b))
                    lanes.append(jnp.concatenate(rows, axis=0))
            return jnp.concatenate(lanes, axis=1)

        even, odd = pick(0), pick(2)
        mean_square = jnp.sum(even * even + odd * odd, axis=1, keepdims=True) * (1.0 / 4096)
        factor = lax.rsqrt(mean_square + EPS)
        edge = jnp.zeros((32, 256), jnp.float32)
        extend = lambda x: jnp.concatenate(
            [edge, (x * factor).astype(jnp.bfloat16).astype(jnp.float32), edge], axis=1
        )
        even, odd = extend(even), extend(odd)
        by = 2304 + 32 * lag
        before = pltpu.roll(odd, by + 1, 1)[:, :2176]
        even, odd = pltpu.roll(even, by, 1)[:, :2176], pltpu.roll(odd, by, 1)[:, :2176]
        e_ref[0] = even
        e_ref[1] = odd - even
        e_ref[2] = before - even

    def build(chunk, rows_ref):
        for q in range(8):
            for kind in (1, 2, 0):
                x = jnp.broadcast_to(e_ref[kind, 8 * chunk + q : 8 * chunk + q + 1, :], (8, 2176))
                for half in range(2):
                    y = [pltpu.roll(x, 16 * half + 8 * e, 1, stride=1, stride_axis=0)[:, 128:] for e in (0, 1)]
                    at = 32 * q + 16 * half
                    rows_ref[kind, at : at + 16, :] = jnp.concatenate(y, 0).astype(jnp.bfloat16)

    def records(q, high, g, k):
        e, near, z, y, x = q // 16, q % 2, q // 2 % 8, 2 * high + g // 4, g % 4
        if k == 3:
            return z_ref[near, z, y, x, e]
        return y_ref[near, y, x, z, k] if e else x_ref[near, x, y, z, k]

    def pieces(n):
        return [(q, high) for q in range(8 * n, 8 * n + 8) for high in (0, 1)]

    def prepare(n):
        totals = []
        for r, (q, high) in enumerate(pieces(n)):
            total = jnp.zeros((16, 128), jnp.float32)
            for g in range(8):
                for lane in range(2):
                    v0 = records(q, high, g, lane).astype(jnp.float32)
                    v1 = records(q, high, g, 2 + lane).astype(jnp.float32)
                    at = 256 * n + 16 * r
                    sums[g, at : at + 16, 128 * lane : 128 * lane + 128] = (v0 + v1).astype(jnp.bfloat16)
                    total += v0 * v0 + v1 * v1
            totals.append(total)
        square = lax.dot_general(
            jnp.ones((8, 128), jnp.float32), jnp.concatenate(totals, 0), CONTRACT,
            precision=lax.Precision.HIGHEST, preferred_element_type=jnp.float32,
        )
        scale_ref[:, 256 * n : 256 * n + 256] = lax.rsqrt(square * (1.0 / 4096) + EPS) * (1.0 / 64)

    def columns(n, kind, g):
        if kind == 0:
            return sums[g, 256 * n : 256 * n + 256, :]
        first = 2 if kind == 1 else 0
        return jnp.concatenate(
            [
                jnp.concatenate([records(q, high, g, first + k) for q, high in pieces(n)], axis=0)
                for k in (0, 1)
            ],
            axis=1,
        )

    def away(chunk, tile):
        return pltpu.make_async_copy(
            stage.at[chunk % 2, tile],
            o_ref.at[pl.ds(8 * chunk, 8), :, pl.ds(128 * tile, 128)],
            sem.at[chunk % 2, tile],
        )

    def multiply(chunk, rows_ref):
        if chunk >= 2:
            for tile in range(8):
                away(chunk - 2, tile).wait()
        for n in range(4):
            if chunk == 0:
                prepare(n)
            products = {}
            for kind in (1, 2, 0):
                right = jnp.concatenate([columns(n, kind, g) for g in range(8)], axis=1)
                products[kind] = lax.dot_general(
                    rows_ref[kind], right, CONTRACT, preferred_element_type=jnp.float32
                )
            for c in range(2):
                cols = slice(256 * n + 128 * c, 256 * n + 128 * c + 128)
                lanes = slice(128 * c, 128 * c + 128)
                for q in range(8):
                    part = slice(32 * q, 32 * q + 32)
                    a = 8 * chunk + q
                    factor = m_ref[a : a + 1, cols].astype(jnp.float32) * scale_ref[0:1, cols]
                    for p in range(2):
                        value = (products[0][part, lanes] + products[1 + p][part, lanes]) * factor
                        stage[chunk % 2, 2 * n + c, q, pl.ds(p, 32, stride=2), :] = value
                away(chunk, 2 * n + c).start()

    fetch = pltpu.make_async_copy(m_hbm, m_ref, m_sem)
    fetch.start()
    shift()
    build(0, even_rows)
    fetch.wait()
    for chunk in range(4):
        now, later = (even_rows, odd_rows) if chunk % 2 == 0 else (odd_rows, even_rows)
        if chunk < 3:
            build(chunk + 1, later)
        multiply(chunk, now)
    for chunk in (2, 3):
        for tile in range(8):
            away(chunk, tile).wait()


def correlate(everyone_x, everyone_y, everyone_z, pair_mask):
    return pl.pallas_call(
        correlate_kernel,
        out_shape=jax.ShapeDtypeStruct((32, 64, 1024), jnp.float32),
        in_specs=[pl.BlockSpec(memory_space=pltpu.VMEM)] * 3 + [pl.BlockSpec(memory_space=pltpu.HBM)],
        out_specs=pl.BlockSpec(memory_space=pl.ANY),
        scratch_shapes=[
            pltpu.VMEM((32, 1024), jnp.int32),
            pltpu.SemaphoreType.DMA,
            pltpu.VMEM((3, 256, 2048), jnp.bfloat16),
            pltpu.VMEM((3, 256, 2048), jnp.bfloat16),
            pltpu.VMEM((8, 1024, 256), jnp.bfloat16),
            pltpu.VMEM((8, 1024), jnp.float32),
            pltpu.VMEM((3, 32, 2176), jnp.float32),
            pltpu.VMEM((2, 8, 8, 64, 128), jnp.float32),
            pltpu.SemaphoreType.DMA((2, 8)),
        ],
        compiler_params=pltpu.CompilerParams(vmem_limit_bytes=40 * 2**20),
    )(everyone_x, everyone_y, everyone_z, pltpu.with_memory_space_constraint(pair_mask, pltpu.HBM))


def body(waves, dest_of, pair_mask):
    return correlate(*gather(waves, dest_of[None, :]), pair_mask)


def solution(mesh):
    in_specs = (P("blk", "lag"), P("blk"), P("blk", None))
    out_specs = P("blk", "lag", None)
    return jax.shard_map(body, mesh=mesh, in_specs=in_specs, out_specs=out_specs, check_vma=False)
```

time: 71.7 us -> 60.2 us (0.84)
  Pallas kernels: 70 us -> 59.9 us
  local copies, waits for them, and re-layouts: 1.45 us -> 0 us
    pallas_call x1, Pallas kernels: 51.9 us -> 41.2 us  [gather(): pl.pallas_call(gather_kernel, out_shape=[pltpu.VMEM((2, 4, 4, 8, 3, 16, 1...]
    unnamed x6 -> x0, local copies, waits for them, and re-layouts: 1.45 us -> none
where the time goes in v1:
time: 60.2 us; the launch traced here: 60.1 us
  Pallas kernels  59.9 us (100%)
    pallas_call x1, Pallas kernels, gather(): pl.pallas_call(gather_kernel, out_shape=[pltpu.VMEM((2, 4, 4, 8, 3, 16, 1...  41.2 us
    pallas_call x1, Pallas kernels, correlate(): pl.pallas_call(correlate_kernel, out_shape=jax.ShapeDtypeStruct((32, 64,...  18.8 us

profile of v1, /device:TPU:1, one launch (start us, length us, event | category | flops | bytes accessed | tf_op | source)
XLA Modules:
  0.0 60.1 jit_solution(10839714206898081095)
XLA Ops:
  0.0 41.2 %shard_map.37 = (bf16[2,4,4,8,3,16,128]{6,5,4,3,2,1,0:T(8,128)(2,1)S(1)}, bf16[2,4,4,8,3,16,128]{6,5,4,3,2,1,0:T(8,128)(2,1)S(1)}, bf16[2,8,4,4,2,16,128]{6,5,4,3,2,1,0:T(8,128)(2,1)S(1)}) custom-call(bf16[32,512]{1,0:T(8,128)(2,1)} %w_hbm.1, s32[1,32]{1,0:T(1,128)} %bitcast.1), custom_call_target="tpu_custom_call" | custom-call | tf_op jit(solution)/shard_map/pallas_call | solution.py:229
  41.2 18.8 %shard_map.38 = f32[32,64,1024]{2,1,0:T(8,128)} custom-call(bf16[2,4,4,8,3,16,128]{6,5,4,3,2,1,0:T(8,128)(2,1)S(1)} %get-tuple-element.8.x_ref, bf16[2,4,4,8,3,16,128]{6,5,4,3,2,1,0:T(8,128)(2,1)S(1)} %get-tuple-element.9.y_ref, bf16[2,8,4,4,2,16,128]{6,5,4,3,2,1,0:T(8,128)(2,1)S(1)} %get-tuple-element.10.z_ref, s32[32,1024]{1,0:T(8,128)} %m_hbm.1), custom_call_target="tpu_custom_call" | custom-call | tf_op jit(solution)/shard_map/pallas_call | solution.py:386

commit v2 on v1

--- a/solution.py
+++ b/solution.py
@@ -13,7 +13,9 @@
 SIZES = {"x": 4, "y": 4, "z": 8}
 
 
-def gather_kernel(w_hbm, d_hbm, held_x, held_y, held_z, w_ref, d_ref, in_sem, s_sem, r_sem):
+def gather_kernel(
+    w_hbm, d_hbm, held_x, held_y, held_z, sum_x, sum_y, squares, w_ref, d_ref, in_sem, s_sem, r_sem
+):
     b, g = lax.axis_index("blk"), lax.axis_index("lag")
     core, cz, yh = b % 2, (b // 2) % 8, b // 16
     yl, cx = g // 4, g % 4
@@ -44,6 +46,7 @@
     ]
     for copy in fetch:
         copy.start()
+    squares[...] = jnp.zeros_like(squares)
     source = lax.broadcasted_iota(jnp.int32, (512, 512), 0)
     target = lax.broadcasted_iota(jnp.int32, (1, 512), 1)
     apart = (source == target % 256 * 2 + target // 256).astype(jnp.bfloat16)
@@ -83,9 +86,9 @@
             device_id=sibling, device_id_type=MESH,
         ).wait_recv()
 
-    def straight(unit, axis, ref_at):
+    def straight(unit, axis, ref_at, places=(2, 1, 3)):
         waits = {}
-        for by in (2, 1, 3) if axis != "z" else (4, 3, 5, 2, 6, 1, 7):
+        for by in places:
             index = start(ref_at(here[axis]), neighbour(axis, by), (unit, 0))
             waits[by] = (ref_at(shifted(axis, -by)), index)
         return waits
@@ -135,11 +138,31 @@
             if way == forward[piece]:
                 launch(axis, piece, way, 2)
 
+    def pass_on(axis, other, held, at, waits):
+        far = {}
+        for by, way, half in ((1, 1, pl.ds(0, 4)), (3, -1, pl.ds(4, 4))):
+            arrive(*waits[by])
+            index = start(held.at[core, at, shifted(other, -way), half], neighbour(other, way), (axis, 0))
+            far[by] = (held.at[core, at, shifted(other, 2), half], index)
+            begin(axis, by)
+        return far
+
     def turn(views):
         joined = jnp.concatenate([ref[index].reshape(256, 128) for ref, index in views], axis=1)
-        turned = jnp.dot(swap, joined, preferred_element_type=jnp.float32).astype(jnp.bfloat16)
-        for k, (ref, index) in enumerate(views):
-            ref[index] = turned[:, 128 * k : 128 * k + 128].reshape(2, 8, 16, 128)
+        turned = jnp.dot(swap, joined, preferred_element_type=jnp.float32)
+        values = [turned[:, 128 * k : 128 * k + 128] for k in range(len(views))]
+        for value, (ref, index) in zip(values, views):
+            ref[index] = value.astype(jnp.bfloat16).reshape(2, 8, 16, 128)
+        return values
+
+    def turn_lines(axis, at, lines):
+        held, sums, e = (held_x, sum_x, 0) if axis == "x" else (held_y, sum_y, 1)
+        values = turn([(held, (slice(None), at, line, slice(None), k)) for line in lines for k in range(3)])
+        for n, line in enumerate(lines):
+            a, b, c = values[3 * n : 3 * n + 3]
+            sums[:, at, line, :, 0] = (a + c).astype(jnp.bfloat16).reshape(2, 8, 16, 128)
+            high = (line if axis == "x" else at) // 2
+            squares[e, high] += a * a + b * b + c * c
 
     def ready(axis, bys):
         for by in bys:
@@ -150,45 +173,71 @@
 
     def arrange(axis, by):
         ready(axis, (by,))
-        held = held_x if axis == "x" else held_y
         at = shifted(axis, by)
         for part in range(2):
-            turn([(held, (slice(None), at, 2 * part + near, slice(None), k)) for near in range(2) for k in range(3)])
+            turn_lines(axis, at, (2 * part, 2 * part + 1))
+
+    def last_line(axis, piece):
+        held, other = (held_x, "y") if axis == "x" else (held_y, "x")
+        return held, shifted(axis, 2), shifted(other, -piece)
+
+    def last_landed(axis, piece):
+        landed(axis, piece, forward[piece], 2)
+        held, at, line = last_line(axis, piece)
+        index = start(held.at[core, at, line], sibling, (axis, 4 + piece))
+        crossing[axis, 4 + piece] = (held.at[1 - core, at, line], index)
+
+    def last_arrange(axis, piece):
+        ready(axis, (4 + piece,))
+        held, at, line = last_line(axis, piece)
+        turn_lines(axis, at, (line,))
 
     def arrange_z():
         ready("z", (0, 1, -1, 2, -2, 3, -3, 4))
         for y in range(4):
-            turn([(held_z, (slice(None), slice(None), y, x, e)) for x in range(4) for e in range(2)])
+            views = [(held_z, (slice(None), slice(None), y, x, e)) for e in range(2) for x in range(4)]
+            values = turn(views)
+            for e in range(2):
+                a, b, c, d = values[4 * e : 4 * e + 4]
+                squares[e, y // 2] += a * a + b * b + c * c + d * d
+
+    def second_sums():
+        for y in range(4):
+            for x in range(4):
+                for sums, held, place, e in ((sum_x, held_x, (x, y), 0), (sum_y, held_y, (y, x), 1)):
+                    near = held[:, place[0], place[1], :, 1].astype(jnp.float32)
+                    far = held_z[:, :, y, x, e].astype(jnp.float32)
+                    sums[:, place[0], place[1], :, 1] = (near + far).astype(jnp.bfloat16)
 
     z_first = straight("z", "x", lambda at: held_z.at[core, cz, cy, at])
-    x_first = straight("x", "z", lambda at: held_x.at[core, cx, cy, at])
-    y_first = straight("y", "z", lambda at: held_y.at[core, cy, cx, at])
+    x_first = straight("x", "z", lambda at: held_x.at[core, cx, cy, at], (4, 3, 5, 2, 6, 1, 7))
+    y_first = straight("y", "z", lambda at: held_y.at[core, cy, cx, at], (4, 3, 5, 2, 6, 1, 7))
     settle(z_first)
     z_mid = straight("z", "y", lambda at: held_z.at[core, cz, at])
     settle(x_first)
-    x_mid = straight("x", "y", lambda at: held_x.at[core, cx, at])
+    x_mid = straight("x", "y", lambda at: held_x.at[core, cx, at], (1, 3))
     begin("x", 0)
     settle(y_first)
-    y_mid = straight("y", "x", lambda at: held_y.at[core, cy, at])
+    y_mid = straight("y", "x", lambda at: held_y.at[core, cy, at], (1, 3))
     begin("y", 0)
     settle(z_mid)
     begin("z", 0)
     begin("z", 1)
     cross("z", 0)
-    for by in (1, 3, 2):
-        arrive(*x_mid[by])
-        begin("x", by)
-    cross("x", 0)
-    for by in (1, 3, 2):
-        arrive(*y_mid[by])
-        begin("y", by)
-    cross("y", 0)
+    far_x = pass_on("x", "y", held_x, cx, x_mid)
+    far_y = pass_on("y", "x", held_y, cy, y_mid)
     z_round(0, 1)
     z_round(1, 1)
     cross("z", 1)
     cross("z", -1)
     xy_round("x", 0)
     xy_round("y", 0)
+    settle(far_x)
+    begin("x", 2)
+    cross("x", 0)
+    settle(far_y)
+    begin("y", 2)
+    cross("y", 0)
     z_round(0, 2)
     z_round(1, 2)
     cross("z", 2)
@@ -209,6 +258,9 @@
     cross("y", -1)
     arrange("x", 0)
     arrange("y", 0)
+    for piece in (0, 1):
+        for axis in "xy":
+            last_landed(axis, piece)
     landed("z", 0, 1, 4)
     landed("z", 1, -1, 4)
     cross("z", 4)
@@ -216,12 +268,17 @@
         arrange(axis, 1)
         arrange(axis, -1)
     for axis in "xy":
-        for piece in (0, 1, 3, 2):
-            landed(axis, piece, forward[piece], 2)
-        cross(axis, 2)
+        last_landed(axis, 3)
+    for piece in (0, 1):
+        for axis in "xy":
+            last_arrange(axis, piece)
+    for axis in "xy":
+        last_landed(axis, 2)
     arrange_z()
-    for axis in "xy":
-        arrange(axis, 2)
+    for piece in (3, 2):
+        for axis in "xy":
+            last_arrange(axis, piece)
+    second_sums()
 
 
 def gather(waves, dest_of):
@@ -232,9 +289,12 @@
             pltpu.VMEM((2, 4, 4, 8, 3, 16, 128), jnp.bfloat16),
             pltpu.VMEM((2, 4, 4, 8, 3, 16, 128), jnp.bfloat16),
             pltpu.VMEM((2, 8, 4, 4, 2, 16, 128), jnp.bfloat16),
+            pltpu.VMEM((2, 4, 4, 8, 2, 16, 128), jnp.bfloat16),
+            pltpu.VMEM((2, 4, 4, 8, 2, 16, 128), jnp.bfloat16),
+            pltpu.VMEM((2, 2, 256, 128), jnp.float32),
         ],
         in_specs=[pl.BlockSpec(memory_space=pltpu.HBM)] * 2,
-        out_specs=[pl.BlockSpec(memory_space=pltpu.VMEM)] * 3,
+        out_specs=[pl.BlockSpec(memory_space=pltpu.VMEM)] * 6,
         scratch_shapes=[
             pltpu.VMEM((32, 512), jnp.bfloat16),
             pltpu.VMEM((1, 32), jnp.int32),
@@ -243,7 +303,7 @@
             pltpu.SemaphoreType.DMA((count,)),
         ],
         compiler_params=pltpu.CompilerParams(
-            collective_id=0, has_side_effects=True, vmem_limit_bytes=16 * 2**20
+            collective_id=0, has_side_effects=True, vmem_limit_bytes=24 * 2**20
         ),
     )(pltpu.with_memory_space_constraint(waves, pltpu.HBM), pltpu.with_memory_space_constraint(dest_of, pltpu.HBM))
 
@@ -251,7 +311,10 @@
 CONTRACT = (((1,), (1,)), ((), ()))
 
 
-def correlate_kernel(x_ref, y_ref, z_ref, m_hbm, o_ref, m_ref, m_sem, even_rows, odd_rows, sums, scale_ref, e_ref, stage, sem):
+def correlate_kernel(
+    x_ref, y_ref, z_ref, sum_x, sum_y, squares, m_hbm, o_ref,
+    m_ref, m_sem, even_rows, odd_rows, scale_ref, e_ref, stage, sem,
+):
     blk, lag = lax.axis_index("blk"), lax.axis_index("lag")
 
     def shift():
@@ -298,6 +361,8 @@
 
     def records(q, high, g, k):
         e, near, z, y, x = q // 16, q % 2, q // 2 % 8, 2 * high + g // 4, g % 4
+        if k >= 4:
+            return sum_y[near, y, x, z, k - 4] if e else sum_x[near, x, y, z, k - 4]
         if k == 3:
             return z_ref[near, z, y, x, e]
         return y_ref[near, y, x, z, k] if e else x_ref[near, x, y, z, k]
@@ -307,16 +372,9 @@
 
     def prepare(n):
         totals = []
-        for r, (q, high) in enumerate(pieces(n)):
-            total = jnp.zeros((16, 128), jnp.float32)
-            for g in range(8):
-                for lane in range(2):
-                    v0 = records(q, high, g, lane).astype(jnp.float32)
-                    v1 = records(q, high, g, 2 + lane).astype(jnp.float32)
-                    at = 256 * n + 16 * r
-                    sums[g, at : at + 16, 128 * lane : 128 * lane + 128] = (v0 + v1).astype(jnp.bfloat16)
-                    total += v0 * v0 + v1 * v1
-            totals.append(total)
+        for q, high in pieces(n):
+            at = 16 * (q % 2 * 8 + q // 2 % 8)
+            totals.append(squares[q // 16, high, at : at + 16, :])
         square = lax.dot_general(
             jnp.ones((8, 128), jnp.float32), jnp.concatenate(totals, 0), CONTRACT,
             precision=lax.Precision.HIGHEST, preferred_element_type=jnp.float32,
@@ -324,9 +382,7 @@
         scale_ref[:, 256 * n : 256 * n + 256] = lax.rsqrt(square * (1.0 / 4096) + EPS) * (1.0 / 64)
 
     def columns(n, kind, g):
-        if kind == 0:
-            return sums[g, 256 * n : 256 * n + 256, :]
-        first = 2 if kind == 1 else 0
+        first = (4, 2, 0)[kind]
         return jnp.concatenate(
             [
                 jnp.concatenate([records(q, high, g, first + k) for q, high in pieces(n)], axis=0)
@@ -382,29 +438,28 @@
             away(chunk, tile).wait()
 
 
-def correlate(everyone_x, everyone_y, everyone_z, pair_mask):
+def correlate(gathered, pair_mask):
     return pl.pallas_call(
         correlate_kernel,
         out_shape=jax.ShapeDtypeStruct((32, 64, 1024), jnp.float32),
-        in_specs=[pl.BlockSpec(memory_space=pltpu.VMEM)] * 3 + [pl.BlockSpec(memory_space=pltpu.HBM)],
+        in_specs=[pl.BlockSpec(memory_space=pltpu.VMEM)] * 6 + [pl.BlockSpec(memory_space=pltpu.HBM)],
         out_specs=pl.BlockSpec(memory_space=pl.ANY),
         scratch_shapes=[
             pltpu.VMEM((32, 1024), jnp.int32),
             pltpu.SemaphoreType.DMA,
             pltpu.VMEM((3, 256, 2048), jnp.bfloat16),
             pltpu.VMEM((3, 256, 2048), jnp.bfloat16),
-            pltpu.VMEM((8, 1024, 256), jnp.bfloat16),
             pltpu.VMEM((8, 1024), jnp.float32),
             pltpu.VMEM((3, 32, 2176), jnp.float32),
             pltpu.VMEM((2, 8, 8, 64, 128), jnp.float32),
             pltpu.SemaphoreType.DMA((2, 8)),
         ],
         compiler_params=pltpu.CompilerParams(vmem_limit_bytes=40 * 2**20),
-    )(everyone_x, everyone_y, everyone_z, pltpu.with_memory_space_constraint(pair_mask, pltpu.HBM))
+    )(*gathered, pltpu.with_memory_space_constraint(pair_mask, pltpu.HBM))
 
 
 def body(waves, dest_of, pair_mask):
-    return correlate(*gather(waves, dest_of[None, :]), pair_mask)
+    return correlate(gather(waves, dest_of[None, :]), pair_mask)
 
 
 def solution(mesh):

time: 60.2 us -> 58.9 us (0.978)
  Pallas kernels: 59.9 us -> 58.5 us
    pallas_call x1, Pallas kernels: 18.8 us -> 17 us  [correlate(): pl.pallas_call(correlate_kernel, out_shape=jax.ShapeDtypeStruct((32, 64,...]
where the time goes in v2:
time: 58.9 us; the launch traced here: 58.7 us
  Pallas kernels  58.5 us (99%)
    pallas_call x1, Pallas kernels, gather(): pl.pallas_call(gather_kernel, out_shape=[pltpu.VMEM((2, 4, 4, 8, 3, 16, 1...  41.5 us
    pallas_call x1, Pallas kernels, correlate(): pl.pallas_call(correlate_kernel, out_shape=jax.ShapeDtypeStruct((32, 64,...  17 us

profile of v2, /device:TPU:1, one launch (start us, length us, event | category | flops | bytes accessed | tf_op | source)
XLA Modules:
  0.0 58.7 jit_solution(7988567542327557742)
XLA Ops:
  0.0 41.5 %shard_map.37 = (bf16[2,4,4,8,3,16,128]{6,5,4,3,2,1,0:T(8,128)(2,1)S(1)}, bf16[2,4,4,8,3,16,128]{6,5,4,3,2,1,0:T(8,128)(2,1)S(1)}, bf16[2,8,4,4,2,16,128]{6,5,4,...) custom-call(bf16[32,512]{1,0:T(8,128)(2,1)} %w_hbm.1, ...), custom_call_target="tpu_custom_call" | custom-call | tf_op jit(solution)/shard_map/pallas_call | solution.py:286
  41.5 17.0 %shard_map.38 = f32[32,64,1024]{2,1,0:T(8,128)} custom-call(bf16[2,4,4,8,3,16,128]{6,5,4,3,2,1,0:T(8,128)(2,1)S(1)} %get-tuple-element.11.x_ref, bf16[2,4,4,8,3,16,128]{6,5,4,3,2,1,0:T(8,128)(2,1)S(1)} %get-tuple-element.12.y_ref, bf16[2,8,4,4,2,16,128]{6,5,4,3,2,1,0:T(8,128)(2,1)S(1)} %get-tuple-element.13.z_ref, ...), custom_call_target="tpu_custom_call" | custom-call | tf_op jit(solution)/shard_map/pallas_call | solution.py:442

commit v3 on v2

--- a/solution.py
+++ b/solution.py
@@ -138,14 +138,11 @@
             if way == forward[piece]:
                 launch(axis, piece, way, 2)
 
-    def pass_on(axis, other, held, at, waits):
-        far = {}
-        for by, way, half in ((1, 1, pl.ds(0, 4)), (3, -1, pl.ds(4, 4))):
+    def pass_on(axis, waits):
+        for by in (1, 3):
             arrive(*waits[by])
-            index = start(held.at[core, at, shifted(other, -way), half], neighbour(other, way), (axis, 0))
-            far[by] = (held.at[core, at, shifted(other, 2), half], index)
             begin(axis, by)
-        return far
+        return {2: waits[2]}
 
     def turn(views):
         joined = jnp.concatenate([ref[index].reshape(256, 128) for ref, index in views], axis=1)
@@ -215,23 +212,23 @@
     settle(z_first)
     z_mid = straight("z", "y", lambda at: held_z.at[core, cz, at])
     settle(x_first)
-    x_mid = straight("x", "y", lambda at: held_x.at[core, cx, at], (1, 3))
+    x_mid = straight("x", "y", lambda at: held_x.at[core, cx, at])
     begin("x", 0)
     settle(y_first)
-    y_mid = straight("y", "x", lambda at: held_y.at[core, cy, at], (1, 3))
+    y_mid = straight("y", "x", lambda at: held_y.at[core, cy, at])
     begin("y", 0)
     settle(z_mid)
     begin("z", 0)
     begin("z", 1)
     cross("z", 0)
-    far_x = pass_on("x", "y", held_x, cx, x_mid)
-    far_y = pass_on("y", "x", held_y, cy, y_mid)
+    far_x = pass_on("x", x_mid)
+    far_y = pass_on("y", y_mid)
+    xy_round("x", 0)
+    xy_round("y", 0)
     z_round(0, 1)
     z_round(1, 1)
     cross("z", 1)
     cross("z", -1)
-    xy_round("x", 0)
-    xy_round("y", 0)
     settle(far_x)
     begin("x", 2)
     cross("x", 0)

time: 58.9 us -> 58.5 us (level)
  no operation moved by 1% of the time
where the time goes in v3:
time: 58.5 us; the launch traced here: 58.4 us
  Pallas kernels  58.2 us (99%)
    pallas_call x1, Pallas kernels, gather(): pl.pallas_call(gather_kernel, out_shape=[pltpu.VMEM((2, 4, 4, 8, 3, 16, 1...  41.2 us
    pallas_call x1, Pallas kernels, correlate(): pl.pallas_call(correlate_kernel, out_shape=jax.ShapeDtypeStruct((32, 64,...  17 us

profile of v3, /device:TPU:1, one launch (start us, length us, event | category | flops | bytes accessed | tf_op | source)
XLA Modules:
  0.0 58.4 jit_solution(6735475534023338596)
XLA Ops:
  0.0 41.2 %shard_map.37 = (bf16[2,4,4,8,3,16,128]{6,5,4,3,2,1,0:T(8,128)(2,1)S(1)}, bf16[2,4,4,8,3,16,128]{6,5,4,3,2,1,0:T(8,128)(2,1)S(1)}, bf16[2,8,4,4,2,16,128]{6,5,4,...) custom-call(bf16[32,512]{1,0:T(8,128)(2,1)} %w_hbm.1, ...), custom_call_target="tpu_custom_call" | custom-call | tf_op jit(solution)/shard_map/pallas_call | solution.py:283
  41.2 17.0 %shard_map.38 = f32[32,64,1024]{2,1,0:T(8,128)} custom-call(bf16[2,4,4,8,3,16,128]{6,5,4,3,2,1,0:T(8,128)(2,1)S(1)} %get-tuple-element.11.x_ref, bf16[2,4,4,8,3,16,128]{6,5,4,3,2,1,0:T(8,128)(2,1)S(1)} %get-tuple-element.12.y_ref, bf16[2,8,4,4,2,16,128]{6,5,4,3,2,1,0:T(8,128)(2,1)S(1)} %get-tuple-element.13.z_ref, ...), custom_call_target="tpu_custom_call" | custom-call | tf_op jit(solution)/shard_map/pallas_call | solution.py:439
